TPU v7x, 1024 devices: a whole 4x4x32 slice. The times are simulated.
1024 devices in a mesh: wide: 64 (over x_lo, z), node: 16 (over x_hi, y, core).
Axes of the slice: x: 4 (x_hi: 2, x_lo: 2; x = x_hi * 2 + x_lo), y: 4, z: 32, core: 2. Of those that a mesh axis runs over, the one named last changes fastest.
Arguments:
- tokens: bfloat16 [131072, 12288], P(('wide', 'node')), may hold values from -24 to 24
- weight_codes: bfloat16 [12288, 128], P('wide', 'node'), may hold values from -4 to 4
- block_scales: bfloat16 [96, 128], P(None, 'node'), may hold values from 0.0029907227 to 0.029907227
- cotangent: bfloat16 [131072, 128], P(('wide', 'node')), may hold values from -0.016479492 to 0.016479492
Outputs:
- projected: bfloat16 [131072, 128], P(('wide', 'node'))
- weight_grad: float32 [12288, 128], P('wide', 'node')
All inputs are finite; a program needn't handle non-finite values.
Results may differ from a plain program's by a relative error of at most 0.015.
Values may be sent and summed in bfloat16 or wider, within the bound.
A program may use at most 64 MiB of HBM per device.

v0:
```python
import jax
import jax.numpy as jnp
from jax import lax
from jax.sharding import PartitionSpec as P

BLOCK = 128


def on_device(tokens, weight_codes, block_scales, cotangent):
    row_codes, row_scales = (
        lax.all_gather(weight_codes, "node", axis=1, tiled=True),
        lax.all_gather(block_scales, "node", axis=1, tiled=True),
    )
    piece = lax.all_gather(row_codes, "wide", axis=0, tiled=True)
    row_index = lax.iota(jnp.int32, piece.shape[0])
    factor = jnp.take(row_scales, row_index // BLOCK, axis=0).astype(jnp.float32)
    dequant = (piece.astype(jnp.float32) * factor).astype(jnp.bfloat16)
    summed = jnp.dot(tokens, dequant, preferred_element_type=jnp.float32)
    projected = summed.astype(jnp.bfloat16)
    partial_value = lax.dot_general(
        tokens, cotangent, (((0,), (0,)), ((), ())), preferred_element_type=jnp.float32
    )
    node_part = lax.psum_scatter(
        partial_value.astype(jnp.bfloat16), "node", scatter_dimension=1, tiled=True
    ).astype(jnp.float32)
    weight_grad = lax.psum_scatter(node_part, "wide", scatter_dimension=0, tiled=True)
    return (projected, weight_grad)


def solution(mesh):
    placed = (
        P(("wide", "node"), None),
        P("wide", "node"),
        P(None, "node"),
        P(("wide", "node"), None),
    )
    return jax.shard_map(
        on_device,
        mesh=mesh,
        in_specs=placed,
        out_specs=(P(("wide", "node"), None), P("wide", "node")),
        check_vma=False,
    )
```

profile of v0, /device:TPU:8, one launch (start us, length us, event | category | flops | bytes accessed | tf_op | source)
XLA Modules:
  0.0 693.3 jit_solution(6954088608012177219)
XLA Ops:
  7.2 0.0 copy-start
  7.2 0.0 reduce-scatter.5.cloned.1.call-start
  7.2 1.8 copy-done
  9.1 3.4 convolution_convert_fusion
  12.5 0.0 reduce-scatter.5.cloned.1.call-update
  12.5 0.0 reduce-scatter.7.cloned.1.call-start
  12.6 138.1 %reduce-scatter.5.cloned.1.call-done = bf16[12288,8]{0,1:T(8,128)(2,1)} async-done(((bf16[12288,128]{0,1:T(8,128)(2,1)}), bf16[12288,8]{0,1:T(8,128)(2,1)}) %reduce-scatter.5.cloned.1.call-update) | async-done | bytes 196624 | tf_op jit(solution)/shard_map/reduce_scatter | solution.py:23
  150.6 4.2 copy.15
  154.8 0.0 copy-start.1
  154.8 0.0 copy-start.2
  154.8 0.0 reduce-scatter.7.cloned.1.call-update
  154.8 0.0 all-gather.2.cloned.1.call-start
  154.9 0.6 copy-done.1
  155.5 19.9 %all_gather.9 = bf16[192,128]{0,1:T(8,128)(2,1)S(1)} all-gather(bf16[192,8]{0,1:T(8,128)(2,1)S(1)} %copy-done.1), channel_id=1, replica_groups=mesh['wide'=64,'node'=16] {'node'}, dimensions={1}, use_global_device_ids=true | all-gather | bytes 52224 | tf_op jit(solution)/shard_map/all_gather | solution.py:11
  175.4 0.7 copy.12
  176.1 0.0 all-gather.2.cloned.1.call-update
  176.1 0.0 copy-done.2
  176.2 21.4 %all_gather.11 = bf16[96,128]{0,1:T(8,128)(2,1)S(1)} all-gather(bf16[96,8]{0,1:T(8,128)(2,1)S(1)} %copy-done.2), channel_id=1, replica_groups=mesh['wide'=64,'node'=16] {'node'}, dimensions={1}, use_global_device_ids=true | all-gather | bytes 26112 | tf_op jit(solution)/shard_map/all_gather | solution.py:12
  197.5 0.1 copy.13
  197.7 43.6 %gather_fusion = bf16[12288,128]{1,0:T(8,128)(2,1)} fusion(bf16[96,128]{1,0:T(8,128)(2,1)S(1)} %copy.13, s32[12288]{0:T(1024)S(1)} %broadcast_clamp_fusion), kind=kCustom, calls=%fused_computation | custom fusion | bytes 6340608 | tf_op jit(solution)/shard_map/jit(_take)/gather | solution.py:16
  241.3 191.1 %reduce-scatter.7.cloned.1.call-done = f32[192,8]{1,0:T(8,128)} async-done(((f32[12288,8]{1,0:T(8,128)}), f32[192,8]{1,0:T(8,128)}) %reduce-scatter.7.cloned.1.call-update) | async-done | bytes 6160
  432.5 1.6 copy.16
  434.0 242.4 %all-gather.2.cloned.1.call-done = bf16[12288,128]{1,0:T(8,128)(2,1)} async-done(((bf16[192,128]{1,0:T(8,128)(2,1)}), bf16[12288,128]{1,0:T(8,128)(2,1)}) %all-gather.2.cloned.1.call-update) | async-done | bytes 3145744 | tf_op jit(solution)/shard_map/all_gather | solution.py:14
  676.5 9.5 %fusion.5 = bf16[128,128]{0,1:T(8,128)(2,1)S(1)} fusion(bf16[128,12288]{1,0:T(8,128)(2,1)S(1)} %copy-done, bf16[12288,128]{1,0:T(8,128)(2,1)} %all-gather.2.cloned.1.call-done, bf16[12288,128]{1,0:T(8,128)(2,1)} %gather_fusion, pred[12288]{0:T(1024)(128)(4,1)S(1)} %fusion.10), kind=kOutput, calls=%fused_computation.8 | convolution fusion | flops 410533888 | bytes 9482240 | tf_op jit(solution)/shard_map/dot_general | solution.py:18
  686.0 0.7 copy.14
  (3 shorter events, 0.1 us)
Async XLA Ops:
  7.2 1.9 copy-start
  7.2 143.4 %reduce-scatter.5.cloned.1.call-start = ((), (), s32[]{:S(2)}) async-start(), calls=%async_computation.3 | async-start | bytes 3342336 | tf_op jit(solution)/shard_map/reduce_scatter | solution.py:23
  12.5 420.0 %reduce-scatter.7.cloned.1.call-start = ((), (), s32[]{:S(2)}) async-start(), calls=%async_computation.4 | async-start | bytes 6389760
  154.8 0.7 copy-start.1
  154.8 21.3 %copy-start.2 = (bf16[96,8]{0,1:T(8,128)(2,1)S(1)}, bf16[96,8]{0,1:T(8,128)(2,1)}, u32[]{:S(2)}) copy-start(bf16[96,8]{0,1:T(8,128)(2,1)} %param.6) | copy-start | bytes 4612
  154.8 521.6 %all-gather.2.cloned.1.call-start = ((), (), s32[]{:S(2)}) async-start(), calls=%async_computation.2 | async-start | bytes 3194880 | tf_op jit(solution)/shard_map/all_gather | solution.py:14
Sparse Core Ops, SparseCore 0:
  14.1 136.4 reduce-scatter.4
  155.0 277.4 reduce-scatter.6
  435.5 240.9 all-gather.1
where the time goes:
time: 694 us; the launch traced here: 693 us
  waiting for transfers between devices  572 us (82%)
  local copies, waits for them, and re-layouts  53.4 us (8%)
  blocking collectives  41.3 us (6%)
  between operations  13.8 us (2%)
  matrix products  13 us (2%)
    all_gather x1, waiting for transfers between devices, on_device(): piece = lax.all_gather(row_codes, 'wide', axis=0, tiled=True)  242 us
    unnamed x4, waiting for transfers between devices  191 us
    reduce_scatter x1, waiting for transfers between devices, on_device(): lax.psum_scatter(partial_value.astype(jnp.bfloat16), 'node', scatter_dime...  138 us
    gather x1, local copies, waits for them, and re-layouts, on_device(): jnp.take(row_scales, row_index // BLOCK, axis=0).astype(jnp.float32)  43.6 us
    all_gather x1, blocking collectives, on_device(): lax.all_gather(block_scales, 'node', axis=1, tiled=True)  21.4 us
    all_gather x1, blocking collectives, on_device(): lax.all_gather(weight_codes, 'node', axis=1, tiled=True)  19.9 us
  transfers between devices with their start and end apart: 3, of which 3 were waited for; matrix products, arithmetic and copies ran while one was open for 7% of the time, Pallas kernels for 0%

commit v1 on v0

v1 whole, which is shorter than its diff:
```python
import jax
import jax.numpy as jnp
from jax import lax
from jax.experimental import pallas as pl
from jax.experimental.pallas import tpu as pltpu
from jax.sharding import PartitionSpec as P

MESH = pl.DeviceIdType.MESH
BF16 = jnp.bfloat16
F32 = jnp.float32
NX = 4
NY = 4
NZ = 32
RES = 8
ROWS = 192
COLS = 16
SPAN = RES * ROWS
PAD = 256
BLOCK = 128


def mod(a, n):
    return lax.rem(a + n, n)


def dot(a, b, ca, cb):
    return lax.dot_general(a, b, (((ca,), (cb,)), ((), ())), preferred_element_type=F32)


def kernel(
    tok_hbm, codes, scales, cot, proj, wg,
    T, C2, cotT, W, G, R1, S1, R2, F0, A, Ar, Zb, Zs, Zr, Zq, Zr2, V, Psum, Pr,
    tl_sem, ts_sem, tr_sem, c_sem, a_sem, v_sem, p_sem,
    z1s_sem, z1r_sem, z2s_sem, z2r_sem,
    r1s_sem, r1r_sem, r2s_sem, r2r_sem,
    a1s_sem, a1r_sem, a2s_sem, a2r_sem,
    q1s_sem, q1r_sem, q2s_sem, q2r_sem,
):
    wide, node = lax.axis_index("wide"), lax.axis_index("node")
    x_lo, z = wide // NZ, lax.rem(wide, NZ)
    x_hi, y, core = node // (2 * NY), lax.rem(node // 2, NY), lax.rem(node, 2)
    x = 2 * x_hi + x_lo
    res, octet = lax.rem(z, RES), z // RES
    odd = lax.rem(z, 2)
    lead = core == z // 16

    def dev(dx=0, dy=0, dz=0, sibling=False):
        xx, yy, zz = lax.rem(x + dx, NX), lax.rem(y + dy, NY), lax.rem(z + dz, NZ)
        cc = 1 - core if sibling else core
        return (lax.rem(xx, 2) * NZ + zz, (xx // 2) * (2 * NY) + yy * 2 + cc)

    def rows(xx, yy):
        return pl.ds(pl.multiple_of(COLS * ((xx // 2) * NY + yy), COLS), COLS)

    def remote(src, dst, send, recv, to):
        return pltpu.make_async_remote_copy(
            src_ref=src, dst_ref=dst, send_sem=send, recv_sem=recv, device_id=to, device_id_type=MESH
        )

    def wait(ref, sem):
        pltpu.make_async_copy(ref, ref, sem).wait()

    near = (1, NZ - 1, 2, NZ - 2, 3, NZ - 3)
    partners = [dev(sibling=True)]
    partners += [dev(dx=k) for k in (1, 2, 3)] + [dev(dy=k) for k in (1, 2, 3)]
    partners += [dev(dz=k) for k in near + (4, NZ - 4)] + [dev(dz=k) for k in (8, 16, 24)]

    barrier = pltpu.get_barrier_semaphore()
    for to in partners:
        pl.semaphore_signal(barrier, inc=1, device_id=to, device_id_type=MESH)

    def columns(xl, half, h):
        return pl.ds(pl.multiple_of(xl * NZ * ROWS + half * 2 * SPAN + h * SPAN, SPAN), SPAN)

    for h in range(2):
        for xl in range(2):
            pltpu.make_async_copy(
                tok_hbm.at[:, columns(xl, core, h)], T.at[xl, h, pl.ds(0, 128)], tl_sem.at[xl, h]
            ).start()

    nb = scales.shape[1]
    block_of = (lax.broadcasted_iota(jnp.int32, (ROWS, nb), 0) + wide * ROWS) // BLOCK
    pick = (block_of == lax.broadcasted_iota(jnp.int32, (ROWS, nb), 1)).astype(BF16)
    factor = dot(scales[...], pick, 1, 1)
    weight = (codes[...].astype(F32) * factor).astype(BF16).astype(F32)
    blank = jnp.zeros((8, PAD - ROWS), F32)
    weight = jnp.where(odd == 1, jnp.concatenate([blank, weight], 1), jnp.concatenate([weight, blank], 1))
    blank = jnp.zeros((8, PAD), F32)
    A[...] = jnp.where(
        core == 0, jnp.concatenate([weight, blank], 0), jnp.concatenate([blank, weight], 0)
    ).astype(BF16)
    eye = (lax.broadcasted_iota(jnp.int32, (128, 128), 0) == lax.broadcasted_iota(jnp.int32, (128, 128), 1)).astype(BF16)

    pl.semaphore_wait(barrier, len(partners))

    sib = dev(sibling=True)
    a_copy = remote(A, Ar, a_sem.at[0], a_sem.at[1], sib)

    @pl.when(jnp.logical_not(lead))
    def _():
        a_copy.start()

    cot_copy = remote(cot, C2, c_sem.at[0], c_sem.at[1], sib)
    cot_copy.start()
    tok_copy = {}
    for h in range(2):
        for xl in range(2):
            tok_copy[xl, h] = remote(
                tok_hbm.at[:, columns(xl, 1 - core, h)],
                T.at[xl, h, pl.ds(128, 128)],
                ts_sem.at[xl, h],
                tr_sem.at[xl, h],
                sib,
            )
            tok_copy[xl, h].start()

    @pl.when(lead)
    def _():
        wait(Ar, a_sem.at[1])
        for h in range(2):

            @pl.when(lax.rem(octet, 2) == h)
            def _():
                Zb[res, h] = A[...] + Ar[...]
                for k in (8, 16, 24):
                    remote(Zb.at[res, h], Zb.at[res, h], z1s_sem, z1r_sem.at[h], dev(dz=k)).start()

    cotT[:, pl.ds(0, 128)] = dot(eye, cot[...], 1, 1).astype(BF16)
    cot_copy.wait_recv()
    cotT[:, pl.ds(128, 128)] = dot(eye, C2[...], 1, 1).astype(BF16)

    def grad(h):
        for xl in range(2):
            wait(T.at[xl, h, pl.ds(0, 128)], tl_sem.at[xl, h])
            tok_copy[xl, h].wait_recv()

            def tile(i, carry):
                at = pl.ds(pl.multiple_of(i * 512, 512), 512)
                G[xl, h, :, at] = dot(cotT[...], T[xl, h, :, at], 1, 0).astype(BF16)
                return carry

            lax.fori_loop(0, SPAN // 512, tile, 0)

    def piece(j, k, h):
        return (lax.rem(x + j, NX), lax.rem(y + k, NY)) if h == 0 else (lax.rem(x + k, NX), lax.rem(y + j, NY))

    def over(k, h):
        return dev(dy=k) if h == 0 else dev(dx=k)

    def send_grad(h):
        for j in (1, 2, 3, 0):
            for k in (1, 3, 2):
                xx, yy = piece(j, k, h)
                remote(
                    G.at[lax.rem(xx, 2), h, rows(xx, yy)], R1.at[h, k - 1, j], r1s_sem, r1r_sem.at[h, k - 1, j], over(k, h)
                ).start()

    grad(0)
    send_grad(0)

    for h in range(2):

        @pl.when(octet != 2 * core + h)
        def _():
            wait(Zb.at[res, h], z1r_sem.at[h])

    for i, k in enumerate(near):
        remote(Zb.at[res], Zb.at[res], z2s_sem, z2r_sem.at[i], dev(dz=k)).start()
    for h, k in ((0, 4), (1, NZ - 4)):
        remote(Zb.at[res, h], Zb.at[res, h], z2s_sem, z2r_sem.at[6 + h], dev(dz=k)).start()

    grad(1)
    send_grad(1)

    for i, k in enumerate(near):
        wait(Zb.at[lax.rem(res + 2 * RES - (k if k < RES else k - NZ), RES)], z2r_sem.at[i])
    for h in range(2):
        wait(Zb.at[lax.rem(res + 4, RES), h], z2r_sem.at[6 + h])
    mine = rows(x, y)
    for h in range(2):
        for j in range(RES // 2):
            at = 384 * j
            W[x_lo, h, mine, at : at + 128] = Zb[2 * j, h, :, 0:128]
            W[x_lo, h, mine, at + 128 : at + 256] = Zb[2 * j, h, :, 128:256] + Zb[2 * j + 1, h, :, 0:128]
            W[x_lo, h, mine, at + 256 : at + 384] = Zb[2 * j + 1, h, :, 128:256]

    for k in (1, 3, 2):
        for h in range(2):
            here = W.at[x_lo, h, mine]
            remote(here, here, a1s_sem, a1r_sem.at[h, k - 1], over(k, 1 - h)).start()

    for h in range(2):
        for j in (1, 2, 3, 0):
            xx, yy = piece(j, 0, h)
            total = G[lax.rem(xx, 2), h, rows(xx, yy)].astype(F32)
            for k in (1, 3, 2):
                wait(R1.at[h, k - 1, j], r1r_sem.at[h, k - 1, j])
                total += R1[h, k - 1, j].astype(F32)
            if j == 0:
                F0[h] = total
            else:
                S1[h, j - 1] = total.astype(BF16)
                remote(S1.at[h, j - 1], R2.at[h, j - 1], r2s_sem, r2r_sem.at[h, j - 1], over(j, 1 - h)).start()

    def origin(j, k, h):
        return (mod(x - j, NX), mod(y - k, NY)) if h == 0 else (mod(x - k, NX), mod(y - j, NY))

    def part(j, k, h):
        xx, yy = origin(j, k, h)
        return W.at[lax.rem(xx, 2), h, rows(xx, yy)]

    for j in (0, 1, 3, 2):
        for h in range(2):
            here = part(j, 0, h)
            if j:
                wait(here, a1r_sem.at[h, j - 1])
            for k in (1, 3, 2):
                remote(here, here, a2s_sem, a2r_sem.at[h, k - 1, j], over(k, h)).start()

    for h in range(2):
        total = F0[h]
        for j in (1, 3, 2):
            wait(R2.at[h, j - 1], r2r_sem.at[h, j - 1])
            total += R2[h, j - 1].astype(F32)
        total = total.astype(BF16)
        for j in range(RES // 2):
            Zs[2 * j, h] = total[:, 384 * j : 384 * j + 256]
            Zs[2 * j + 1, h] = total[:, 384 * j + 128 : 384 * j + 384]

    for i, k in enumerate(near):
        remote(Zs.at[lax.rem(res + k, RES)], Zr.at[i], q1s_sem, q1r_sem.at[i], dev(dz=k)).start()
    for h, k in ((0, 4), (1, NZ - 4)):
        remote(Zs.at[lax.rem(res + 4, RES), h], Zr.at[6, h], q1s_sem, q1r_sem.at[6 + h], dev(dz=k)).start()
    for i in range(6):
        wait(Zr.at[i], q1r_sem.at[i])
    for h in range(2):
        wait(Zr.at[6, h], q1r_sem.at[6 + h])
    total = Zs[res].astype(F32)
    for i in range(7):
        total += Zr[i].astype(F32)
    Zq[...] = total.astype(BF16)

    for h in range(2):
        hop = lax.rem(2 * core + h - octet + 4, 4)
        for k in (1, 2, 3):

            @pl.when(hop == k)
            def _():
                remote(Zq.at[h], Zr2.at[k - 1], q2s_sem.at[h], q2r_sem.at[k - 1], dev(dz=8 * k)).start()

    v_copy = remote(V, V, v_sem.at[0], v_sem.at[1], sib)

    @pl.when(lead)
    def _():
        total = Zq[lax.rem(octet, 2)].astype(F32)
        for k in (1, 2, 3):
            wait(Zr2.at[k - 1], q2r_sem.at[k - 1])
            total += Zr2[k - 1].astype(F32)
        V[...] = total
        v_copy.start()

    acc = None
    for h in range(2):
        for k in (1, 3, 2):
            for j in range(4):
                wait(part(j, k, h), a2r_sem.at[h, k - 1, j])
        for xl in range(2):
            term = dot(T[xl, h], W[xl, h], 1, 1)
            acc = term if acc is None else acc + term
    Psum[...] = acc
    p_copy = remote(Psum.at[pl.ds(128, 128)], Pr, p_sem.at[0], p_sem.at[1], sib)
    p_copy.start()

    @pl.when(jnp.logical_not(lead))
    def _():
        v_copy.wait_recv()

    picked = jnp.where(core == 0, V[0:8], V[8:16])
    picked = jnp.where(odd == 1, picked[:, 64:PAD], picked[:, 0:ROWS])
    wg[...] = picked

    p_copy.wait_recv()
    proj[...] = (Psum[0:128] + Pr[...]).astype(BF16)

    p_copy.wait_send()
    cot_copy.wait_send()
    for copy in tok_copy.values():
        copy.wait_send()

    @pl.when(lead)
    def _():
        v_copy.wait_send()
        wait(Zr2, z1s_sem)

    @pl.when(jnp.logical_not(lead))
    def _():
        a_copy.wait_send()

    wait(Zr, z2s_sem)
    wait(Zr, q1s_sem)
    wait(R1, r1s_sem)
    wait(R1, a2s_sem)
    wait(R2, r2s_sem)
    wait(R2, a1s_sem)
    for h in range(2):

        @pl.when(octet != 2 * core + h)
        def _():
            wait(Zq.at[h], q2s_sem.at[h])


def on_device(tokens, weight_codes, block_scales, cotangent):
    vmem = pl.BlockSpec(memory_space=pltpu.VMEM)
    dma = pltpu.SemaphoreType.DMA
    projected, turned = pl.pallas_call(
        kernel,
        out_shape=(
            jax.ShapeDtypeStruct((128, 128), BF16),
            jax.ShapeDtypeStruct((8, ROWS), F32),
        ),
        in_specs=[pl.BlockSpec(memory_space=pl.ANY), vmem, vmem, vmem],
        out_specs=(vmem, vmem),
        scratch_shapes=[
            pltpu.VMEM((2, 2, 256, SPAN), BF16),
            pltpu.VMEM((128, 128), BF16),
            pltpu.VMEM((128, 256), BF16),
            pltpu.VMEM((2, 2, 128, SPAN), BF16),
            pltpu.VMEM((2, 2, 128, SPAN), BF16),
            pltpu.VMEM((2, 3, 4, COLS, SPAN), BF16),
            pltpu.VMEM((2, 3, COLS, SPAN), BF16),
            pltpu.VMEM((2, 3, COLS, SPAN), BF16),
            pltpu.VMEM((2, COLS, SPAN), F32),
            pltpu.VMEM((COLS, PAD), BF16),
            pltpu.VMEM((COLS, PAD), BF16),
            pltpu.VMEM((RES, 2, COLS, PAD), BF16),
            pltpu.VMEM((RES, 2, COLS, PAD), BF16),
            pltpu.VMEM((7, 2, COLS, PAD), BF16),
            pltpu.VMEM((2, COLS, PAD), BF16),
            pltpu.VMEM((3, COLS, PAD), BF16),
            pltpu.VMEM((COLS, PAD), F32),
            pltpu.VMEM((256, 128), F32),
            pltpu.VMEM((128, 128), F32),
            dma((2, 2)),
            dma((2, 2)),
            dma((2, 2)),
            dma((2,)),
            dma((2,)),
            dma((2,)),
            dma((2,)),
            dma,
            dma((2,)),
            dma,
            dma((8,)),
            dma,
            dma((2, 3, 4)),
            dma,
            dma((2, 3)),
            dma,
            dma((2, 3)),
            dma,
            dma((2, 3, 4)),
            dma,
            dma((8,)),
            dma((2,)),
            dma((3,)),
        ],
        compiler_params=pltpu.CompilerParams(
            collective_id=0, has_side_effects=True, vmem_limit_bytes=60 * 1024 * 1024
        ),
    )(tokens, weight_codes.T, block_scales.T, cotangent)
    return projected, turned.T


def solution(mesh):
    placed = (
        P(("wide", "node"), None),
        P("wide", "node"),
        P(None, "node"),
        P(("wide", "node"), None),
    )
    return jax.shard_map(
        on_device,
        mesh=mesh,
        in_specs=placed,
        out_specs=(P(("wide", "node"), None), P("wide", "node")),
        check_vma=False,
    )
```

time: 694 us -> 83.1 us (0.12)
  the two profiles are of different devices: /device:TPU:8 before, /device:TPU:1 now
where the time goes in v1:
time: 83.1 us; the launch traced here: 82.8 us
  Pallas kernels  79.4 us (96%)
  local copies, waits for them, and re-layouts  2.67 us (3%)
    pallas_call x1, Pallas kernels, on_device(): pl.pallas_call(kernel, out_shape=(jax.ShapeDtypeStruct((128, 128), BF16),...  79.4 us
    unnamed x2, local copies, waits for them, and re-layouts  2.67 us

profile of v1, /device:TPU:1, one launch (start us, length us, event | category | flops | bytes accessed | tf_op | source)
XLA Modules:
  0.0 82.8 jit_solution(15874604977940328548)
XLA Ops:
  0.6 79.4 %shard_map.59 = (bf16[128,128]{1,0:T(8,128)(2,1)}, f32[8,192]{1,0:T(8,128)}) custom-call(bf16[128,12288]{1,0:T(8,128)(2,1)} %tok_hbm.1, bf16[8,192]{1,0:T(8,128)(2,1)} %bitcast.4, bf16[8,96]{1,0:T(8,128)(2,1)} %bitcast.5, bf16[128,128]{1,0:T(8,128)(2,1)} %cot.1), custom_call_target="tpu_custom_call" | custom-call | tf_op jit(solution)/shard_map/pallas_call | solution.py:315
  80.1 1.4 %copy.8 = bf16[128,128]{1,0:T(8,128)(2,1)} copy(bf16[128,128]{1,0:T(8,128)(2,1)} %get-tuple-element.8) | data formatting | bytes 65536
  81.5 1.3 %copy.9 = f32[192,8]{0,1:T(8,128)} copy(f32[192,8]{0,1:T(8,128)} %bitcast.3) | data formatting | bytes 12288

commit v2 on v1

v2 whole, which is shorter than its diff:
```python
import jax
import jax.numpy as jnp
from jax import lax
from jax.experimental import pallas as pl
from jax.experimental.pallas import tpu as pltpu
from jax.sharding import PartitionSpec as P

MESH = pl.DeviceIdType.MESH
BF16 = jnp.bfloat16
F32 = jnp.float32
NX = 4
NY = 4
NZ = 32
RES = 8
ROWS = 192
COLS = 16
SPAN = RES * ROWS
PAD = 256
BLOCK = 128


def mod(a, n):
    return lax.rem(a + n, n)


def dot(a, b, ca, cb):
    return lax.dot_general(a, b, (((ca,), (cb,)), ((), ())), preferred_element_type=F32)


def kernel(
    tok_hbm, codes, scales, cot, proj, wg,
    T, C2, cotT, W, G, R1, S1, R2, F0, A, Ar, Zb, Zs, Zr, Zq, Zr2, Psum, Pr,
    tl_sem, ts_sem, tr_sem, c_sem, a_sem, v_sem, p_sem,
    n_sem, z1s_sem, z1r_sem, z2s_sem, z2r_sem,
    r1s_sem, r1r_sem, r2s_sem, r2r_sem,
    a1s_sem, a1r_sem, a2s_sem, a2r_sem,
    q1s_sem, q1r_sem, q2s_sem, q2r_sem,
):
    wide, node = lax.axis_index("wide"), lax.axis_index("node")
    x_lo, z = wide // NZ, lax.rem(wide, NZ)
    x_hi, y, core = node // (2 * NY), lax.rem(node // 2, NY), lax.rem(node, 2)
    x = 2 * x_hi + x_lo
    res, octet = lax.rem(z, RES), z // RES
    odd = lax.rem(z, 2)
    lead = core == z // 16

    def dev(dx=0, dy=0, dz=0, sibling=False):
        xx, yy, zz = lax.rem(x + dx, NX), lax.rem(y + dy, NY), lax.rem(z + dz, NZ)
        cc = 1 - core if sibling else core
        return (lax.rem(xx, 2) * NZ + zz, (xx // 2) * (2 * NY) + yy * 2 + cc)

    def rows(xx, yy):
        return pl.ds(pl.multiple_of(COLS * ((xx // 2) * NY + yy), COLS), COLS)

    def remote(src, dst, send, recv, to):
        return pltpu.make_async_remote_copy(
            src_ref=src, dst_ref=dst, send_sem=send, recv_sem=recv, device_id=to, device_id_type=MESH
        )

    def wait(ref, sem):
        pltpu.make_async_copy(ref, ref, sem).wait()

    near = (3, NZ - 3, 2, NZ - 2, 1, NZ - 1)
    partners = [dev(sibling=True)]
    partners += [dev(dx=k) for k in (1, 2, 3)] + [dev(dy=k) for k in (1, 2, 3)]
    partners += [dev(dz=k) for k in near + (4, NZ - 4)]

    barrier = pltpu.get_barrier_semaphore()
    for to in partners:
        pl.semaphore_signal(barrier, inc=1, device_id=to, device_id_type=MESH)

    def columns(xl, half, h):
        return pl.ds(pl.multiple_of(xl * NZ * ROWS + half * 2 * SPAN + h * SPAN, SPAN), SPAN)

    chunks = [(lax.rem(x_lo + 1 + a, 2), a, h) for a in range(2) for h in range(2)]
    for xl, a, h in chunks:
        pltpu.make_async_copy(
            tok_hbm.at[:, columns(xl, core, h)], T.at[xl, h, pl.ds(0, 128)], tl_sem.at[a, h]
        ).start()

    nb = scales.shape[1]
    block_of = (lax.broadcasted_iota(jnp.int32, (ROWS, nb), 0) + wide * ROWS) // BLOCK
    pick = (block_of == lax.broadcasted_iota(jnp.int32, (ROWS, nb), 1)).astype(BF16)
    factor = dot(scales[...], pick, 1, 1)
    weight = (codes[...].astype(F32) * factor).astype(BF16).astype(F32)
    blank = jnp.zeros((8, PAD - ROWS), F32)
    weight = jnp.where(odd == 1, jnp.concatenate([blank, weight], 1), jnp.concatenate([weight, blank], 1))
    blank = jnp.zeros((8, PAD), F32)
    A[...] = jnp.where(
        core == 0, jnp.concatenate([weight, blank], 0), jnp.concatenate([blank, weight], 0)
    ).astype(BF16)
    eye = (lax.broadcasted_iota(jnp.int32, (128, 128), 0) == lax.broadcasted_iota(jnp.int32, (128, 128), 1)).astype(BF16)

    pl.semaphore_wait(barrier, len(partners))
    for k in (4, NZ - 4):
        pl.semaphore_signal(n_sem, inc=1, device_id=dev(dz=k), device_id_type=MESH)

    sib = dev(sibling=True)
    a_copy = remote(A, Ar, a_sem.at[0], a_sem.at[1], sib)

    @pl.when(jnp.logical_not(lead))
    def _():
        a_copy.start()

    cot_copy = remote(cot, C2, c_sem.at[0], c_sem.at[1], sib)
    cot_copy.start()
    tok_copy = {}
    for xl, a, h in chunks:
        tok_copy[a, h] = remote(
            tok_hbm.at[:, columns(xl, 1 - core, h)],
            T.at[xl, h, pl.ds(128, 128)],
            ts_sem.at[a, h],
            tr_sem.at[a, h],
            sib,
        )
        tok_copy[a, h].start()

    pl.semaphore_wait(n_sem, 2)

    def onward(h, i, k):
        here = Zb.at[res, h]
        return remote(here, here, z1s_sem.at[h, i], z1r_sem.at[h], dev(dz=k))

    place = [lax.rem(octet - 2 * core - h + 4, 4) for h in range(2)]

    @pl.when(lead)
    def _():
        wait(Ar, a_sem.at[1])
        for h in range(2):

            @pl.when(place[h] == 0)
            def _():
                Zb[res, h] = A[...] + Ar[...]
                onward(h, 0, 8).start()
                onward(h, 1, 24).start()

    cotT[:, pl.ds(0, 128)] = dot(eye, cot[...], 1, 1).astype(BF16)
    cot_copy.wait_recv()
    cotT[:, pl.ds(128, 128)] = dot(eye, C2[...], 1, 1).astype(BF16)

    def grad(xl, a, h):
        wait(T.at[xl, h, pl.ds(0, 128)], tl_sem.at[a, h])
        tok_copy[a, h].wait_recv()

        def tile(i, carry):
            at = pl.ds(pl.multiple_of(i * 512, 512), 512)
            G[xl, h, :, at] = dot(cotT[...], T[xl, h, :, at], 1, 0).astype(BF16)
            return carry

        lax.fori_loop(0, SPAN // 512, tile, 0)

    def piece(j, k, h):
        return (lax.rem(x + j, NX), lax.rem(y + k, NY)) if h == 0 else (lax.rem(x + k, NX), lax.rem(y + j, NY))

    def over(k, h):
        return dev(dy=k) if h == 0 else dev(dx=k)

    def send_grad(a, h):
        if h == 0:
            pairs = [(j, k) for j in ((1, 3), (2, 0))[a] for k in (2, 1, 3)]
        else:
            pairs = [(j, k) for j in (1, 3, 2, 0) for k in ((1, 3), (2,))[a]]
        for j, k in pairs:
            xx, yy = piece(j, k, h)
            remote(
                G.at[lax.rem(xx, 2), h, rows(xx, yy)], R1.at[h, k - 1, j], r1s_sem, r1r_sem.at[h, k - 1, j], over(k, h)
            ).start()

    for xl, a, h in chunks:
        grad(xl, a, h)
        send_grad(a, h)

    for h in range(2):

        @pl.when(place[h] == 1)
        def _():
            wait(Zb.at[res, h], z1r_sem.at[h])
            onward(h, 0, 8).start()

    for h in range(2):

        @pl.when(place[h] >= 2)
        def _():
            wait(Zb.at[res, h], z1r_sem.at[h])

    for h, k in ((0, 4), (1, NZ - 4)):
        remote(Zb.at[res, h], Zb.at[res, h], z2s_sem, z2r_sem.at[6 + h], dev(dz=k)).start()
    for i, k in enumerate(near):
        remote(Zb.at[res], Zb.at[res], z2s_sem, z2r_sem.at[i], dev(dz=k)).start()

    for h in range(2):
        for j in (1, 3, 2, 0):
            xx, yy = piece(j, 0, h)
            total = G[lax.rem(xx, 2), h, rows(xx, yy)].astype(F32)
            for k in (1, 3, 2):
                wait(R1.at[h, k - 1, j], r1r_sem.at[h, k - 1, j])
                total += R1[h, k - 1, j].astype(F32)
            if j == 0:
                F0[h] = total
            else:
                S1[h, j - 1] = total.astype(BF16)
                remote(S1.at[h, j - 1], R2.at[h, j - 1], r2s_sem, r2r_sem.at[h, j - 1], over(j, 1 - h)).start()

    for i, k in enumerate(near):
        wait(Zb.at[lax.rem(res + 2 * RES - (k if k < RES else k - NZ), RES)], z2r_sem.at[i])
    for h in range(2):
        wait(Zb.at[lax.rem(res + 4, RES), h], z2r_sem.at[6 + h])
    mine = rows(x, y)
    for h in range(2):
        for j in range(RES // 2):
            at = 384 * j
            W[x_lo, h, mine, at : at + 128] = Zb[2 * j, h, :, 0:128]
            W[x_lo, h, mine, at + 128 : at + 256] = Zb[2 * j, h, :, 128:256] + Zb[2 * j + 1, h, :, 0:128]
            W[x_lo, h, mine, at + 256 : at + 384] = Zb[2 * j + 1, h, :, 128:256]

    for k in (1, 3, 2):
        for h in range(2):
            here = W.at[x_lo, h, mine]
            remote(here, here, a1s_sem, a1r_sem.at[h, k - 1], over(k, 1 - h)).start()

    for h in range(2):
        total = F0[h]
        for j in (1, 3, 2):
            wait(R2.at[h, j - 1], r2r_sem.at[h, j - 1])
            total += R2[h, j - 1].astype(F32)
        total = total.astype(BF16)
        for j in range(RES // 2):
            Zs[2 * j, h] = total[:, 384 * j : 384 * j + 256]
            Zs[2 * j + 1, h] = total[:, 384 * j + 128 : 384 * j + 384]

    for h, k in ((0, 4), (1, NZ - 4)):
        remote(Zs.at[lax.rem(res + 4, RES), h], Zr.at[6, h], q1s_sem, q1r_sem.at[6 + h], dev(dz=k)).start()
    for i, k in enumerate(near):
        remote(Zs.at[lax.rem(res + k, RES)], Zr.at[i], q1s_sem, q1r_sem.at[i], dev(dz=k)).start()
    def origin(j, k, h):
        return (mod(x - j, NX), mod(y - k, NY)) if h == 0 else (mod(x - k, NX), mod(y - j, NY))

    def part(j, k, h):
        xx, yy = origin(j, k, h)
        return W.at[lax.rem(xx, 2), h, rows(xx, yy)]

    for j in (0, 1, 3, 2):
        for h in range(2):
            here = part(j, 0, h)
            if j:
                wait(here, a1r_sem.at[h, j - 1])
            for k in (1, 3, 2):
                remote(here, here, a2s_sem, a2r_sem.at[h, k - 1, j], over(k, h)).start()

    for i in range(6):
        wait(Zr.at[i], q1r_sem.at[i])
    for h in range(2):
        wait(Zr.at[6, h], q1r_sem.at[6 + h])
    total = Zs[res].astype(F32)
    for i in range(7):
        total += Zr[i].astype(F32)
    Zq[...] = total.astype(BF16)

    def out_of(h, k, both):
        return remote(
            Zq.at[h], Zr2.at[k - 1], q2s_sem.at[h, both], q2r_sem.at[k - 1], dev(dz=8 * k, sibling=both == 1)
        )

    for h in range(2):
        for k in (2, 1, 3):

            @pl.when(place[h] == 4 - k)
            def _():
                out_of(h, k, 0).start()
                out_of(h, k, 1).start()

    own = Zq.at[lax.rem(octet, 2)]
    v_copy = remote(own, Zr2.at[3], v_sem.at[0], v_sem.at[1], sib)

    @pl.when(lead)
    def _():
        v_copy.start()
        Zr2[3] = own[...]

    acc = None
    for h in range(2):
        for k in (1, 3, 2):
            for j in range(4):
                wait(part(j, k, h), a2r_sem.at[h, k - 1, j])
        for xl in range(2):
            term = dot(T[xl, h], W[xl, h], 1, 1)
            acc = term if acc is None else acc + term
    Psum[...] = acc
    p_copy = remote(Psum.at[pl.ds(128, 128)], Pr, p_sem.at[0], p_sem.at[1], sib)
    p_copy.start()

    @pl.when(jnp.logical_not(lead))
    def _():
        v_copy.wait_recv()

    total = Zr2[3].astype(F32)
    for k in (1, 2, 3):
        wait(Zr2.at[k - 1], q2r_sem.at[k - 1])
        total += Zr2[k - 1].astype(F32)
    picked = jnp.where(core == 0, total[0:8], total[8:16])
    wg[...] = jnp.where(odd == 1, picked[:, 64:PAD], picked[:, 0:ROWS])

    p_copy.wait_recv()
    proj[...] = (Psum[0:128] + Pr[...]).astype(BF16)

    p_copy.wait_send()
    cot_copy.wait_send()
    for copy in tok_copy.values():
        copy.wait_send()

    @pl.when(lead)
    def _():
        v_copy.wait_send()

    @pl.when(jnp.logical_not(lead))
    def _():
        a_copy.wait_send()

    wait(Zr, z2s_sem)
    wait(Zr, q1s_sem)
    wait(R1, r1s_sem)
    wait(R1, a2s_sem)
    wait(R2, r2s_sem)
    wait(R2, a1s_sem)
    for h in range(2):

        @pl.when(place[h] != 0)
        def _():
            wait(Zq.at[h], q2s_sem.at[h, 0])
            wait(Zq.at[h], q2s_sem.at[h, 1])

        @pl.when(place[h] == 0)
        def _():
            wait(Zb.at[res, h], z1s_sem.at[h, 1])

        @pl.when(place[h] <= 1)
        def _():
            wait(Zb.at[res, h], z1s_sem.at[h, 0])


def on_device(tokens, weight_codes, block_scales, cotangent):
    vmem = pl.BlockSpec(memory_space=pltpu.VMEM)
    dma = pltpu.SemaphoreType.DMA
    projected, turned = pl.pallas_call(
        kernel,
        out_shape=(
            jax.ShapeDtypeStruct((128, 128), BF16),
            jax.ShapeDtypeStruct((8, ROWS), F32),
        ),
        in_specs=[pl.BlockSpec(memory_space=pltpu.HBM), vmem, vmem, vmem],
        out_specs=(vmem, vmem),
        scratch_shapes=[
            pltpu.VMEM((2, 2, 256, SPAN), BF16),
            pltpu.VMEM((128, 128), BF16),
            pltpu.VMEM((128, 256), BF16),
            pltpu.VMEM((2, 2, 128, SPAN), BF16),
            pltpu.VMEM((2, 2, 128, SPAN), BF16),
            pltpu.VMEM((2, 3, 4, COLS, SPAN), BF16),
            pltpu.VMEM((2, 3, COLS, SPAN), BF16),
            pltpu.VMEM((2, 3, COLS, SPAN), BF16),
            pltpu.VMEM((2, COLS, SPAN), F32),
            pltpu.VMEM((COLS, PAD), BF16),
            pltpu.VMEM((COLS, PAD), BF16),
            pltpu.VMEM((RES, 2, COLS, PAD), BF16),
            pltpu.VMEM((RES, 2, COLS, PAD), BF16),
            pltpu.VMEM((7, 2, COLS, PAD), BF16),
            pltpu.VMEM((2, COLS, PAD), BF16),
            pltpu.VMEM((4, COLS, PAD), BF16),
            pltpu.VMEM((256, 128), F32),
            pltpu.VMEM((128, 128), F32),
            dma((2, 2)),
            dma((2, 2)),
            dma((2, 2)),
            dma((2,)),
            dma((2,)),
            dma((2,)),
            dma((2,)),
            pltpu.SemaphoreType.REGULAR,
            dma((2, 2)),
            dma((2,)),
            dma,
            dma((8,)),
            dma,
            dma((2, 3, 4)),
            dma,
            dma((2, 3)),
            dma,
            dma((2, 3)),
            dma,
            dma((2, 3, 4)),
            dma,
            dma((8,)),
            dma((2, 2)),
            dma((3,)),
        ],
        compiler_params=pltpu.CompilerParams(
            collective_id=0, has_side_effects=True, vmem_limit_bytes=52 * 1024 * 1024
        ),
    )(tokens, weight_codes.T, block_scales.T, cotangent)
    return projected, turned.T


def solution(mesh):
    placed = (
        P(("wide", "node"), None),
        P("wide", "node"),
        P(None, "node"),
        P(("wide", "node"), None),
    )
    return jax.shard_map(
        on_device,
        mesh=mesh,
        in_specs=placed,
        out_specs=(P(("wide", "node"), None), P("wide", "node")),
        check_vma=False,
    )
```

time: 83.1 us -> 65.9 us (0.79)
  Pallas kernels: 79.4 us -> 61.7 us
    pallas_call x1, Pallas kernels: 79.4 us -> 61.7 us  [on_device(): pl.pallas_call(kernel, out_shape=(jax.ShapeDtypeStruct((128, 128), BF16),...]
    unnamed x2 -> x8, local copies, waits for them, and re-layouts: 2.67 us -> 3.33 us
where the time goes in v2:
time: 65.9 us; the launch traced here: 65.7 us
  Pallas kernels  61.7 us (94%)
  local copies, waits for them, and re-layouts  3.33 us (5%)
    pallas_call x1, Pallas kernels, on_device(): pl.pallas_call(kernel, out_shape=(jax.ShapeDtypeStruct((128, 128), BF16),...  61.7 us
    unnamed x8, local copies, waits for them, and re-layouts  3.33 us

profile of v2, /device:TPU:1, one launch (start us, length us, event | category | flops | bytes accessed | tf_op | source)
XLA Modules:
  0.0 65.7 jit_solution(3343277142344543516)
XLA Ops:
  0.6 0.0 copy-start
  0.6 0.7 %copy-done = bf16[128,128]{1,0:T(8,128)(2,1)S(1)} copy-done((bf16[128,128]{1,0:T(8,128)(2,1)S(1)}, bf16[128,128]{1,0:T(8,128)(2,1)}, u32[]{:S(2)}) %copy-start) | copy-done | bytes 32792
  1.4 0.0 copy-start.1
  1.4 0.7 %copy-done.1 = bf16[192,8]{0,1:T(8,128)(2,1)S(1)} copy-done((bf16[192,8]{0,1:T(8,128)(2,1)S(1)}, bf16[192,8]{0,1:T(8,128)(2,1)}, u32[]{:S(2)}) %copy-start.1) | copy-done | bytes 3096
  2.1 0.0 copy-start.2
  2.1 0.7 %copy-done.2 = bf16[96,8]{0,1:T(8,128)(2,1)S(1)} copy-done((bf16[96,8]{0,1:T(8,128)(2,1)S(1)}, bf16[96,8]{0,1:T(8,128)(2,1)}, u32[]{:S(2)}) %copy-start.2) | copy-done | bytes 1560
  2.8 61.7 %shard_map.59 = (bf16[128,128]{1,0:T(8,128)(2,1)S(1)}, f32[8,192]{1,0:T(8,128)S(1)}) custom-call(bf16[128,12288]{1,0:T(8,128)(2,1)} %tok_hbm.1, bf16[8,192]{1,0:T(8,128)(2,1)S(1)} %bitcast.4, bf16[8,96]{1,0:T(8,128)(2,1)S(1)} %bitcast.5, bf16[128,128]{1,0:T(8,128)(2,1)S(1)} %copy-done), custom_call_target="tpu_custom_call" | custom-call | tf_op jit(solution)/shard_map/pallas_call | solution.py:344
  64.5 0.6 copy.8
  65.1 0.6 copy.9
Async XLA Ops:
  0.6 0.8 %copy-start = (bf16[128,128]{1,0:T(8,128)(2,1)S(1)}, bf16[128,128]{1,0:T(8,128)(2,1)}, u32[]{:S(2)}) copy-start(bf16[128,128]{1,0:T(8,128)(2,1)} %cot.1) | copy-start | bytes 98308
  1.4 0.7 %copy-start.1 = (bf16[192,8]{0,1:T(8,128)(2,1)S(1)}, bf16[192,8]{0,1:T(8,128)(2,1)}, u32[]{:S(2)}) copy-start(bf16[192,8]{0,1:T(8,128)(2,1)} %param.5) | copy-start | bytes 9220
  2.1 0.7 %copy-start.2 = (bf16[96,8]{0,1:T(8,128)(2,1)S(1)}, bf16[96,8]{0,1:T(8,128)(2,1)}, u32[]{:S(2)}) copy-start(bf16[96,8]{0,1:T(8,128)(2,1)} %param.6) | copy-start | bytes 4612

commit v3 on v2

--- a/solution.py
+++ b/solution.py
@@ -28,9 +28,10 @@
 
 
 def kernel(
-    tok_hbm, codes, scales, cot, proj, wg,
+    tok_hbm, codes_hbm, scales_hbm, cot_hbm, proj, wg,
+    codes, scales, cot,
     T, C2, cotT, W, G, R1, S1, R2, F0, A, Ar, Zb, Zs, Zr, Zq, Zr2, Psum, Pr,
-    tl_sem, ts_sem, tr_sem, c_sem, a_sem, v_sem, p_sem,
+    in_sem, tl_sem, ts_sem, tr_sem, c_sem, a_sem, v_sem, p_sem,
     n_sem, z1s_sem, z1r_sem, z2s_sem, z2r_sem,
     r1s_sem, r1r_sem, r2s_sem, r2r_sem,
     a1s_sem, a1r_sem, a2s_sem, a2r_sem,
@@ -69,6 +70,13 @@
     for to in partners:
         pl.semaphore_signal(barrier, inc=1, device_id=to, device_id_type=MESH)
 
+    loads = [
+        pltpu.make_async_copy(src, dst, in_sem.at[i])
+        for i, (src, dst) in enumerate(((codes_hbm, codes), (scales_hbm, scales), (cot_hbm, cot)))
+    ]
+    for load in loads:
+        load.start()
+
     def columns(xl, half, h):
         return pl.ds(pl.multiple_of(xl * NZ * ROWS + half * 2 * SPAN + h * SPAN, SPAN), SPAN)
 
@@ -78,6 +86,8 @@
             tok_hbm.at[:, columns(xl, core, h)], T.at[xl, h, pl.ds(0, 128)], tl_sem.at[a, h]
         ).start()
 
+    loads[0].wait()
+    loads[1].wait()
     nb = scales.shape[1]
     block_of = (lax.broadcasted_iota(jnp.int32, (ROWS, nb), 0) + wide * ROWS) // BLOCK
     pick = (block_of == lax.broadcasted_iota(jnp.int32, (ROWS, nb), 1)).astype(BF16)
@@ -102,7 +112,7 @@
     def _():
         a_copy.start()
 
-    cot_copy = remote(cot, C2, c_sem.at[0], c_sem.at[1], sib)
+    cot_copy = remote(cot_hbm, C2, c_sem.at[0], c_sem.at[1], sib)
     cot_copy.start()
     tok_copy = {}
     for xl, a, h in chunks:
@@ -115,6 +125,46 @@
         )
         tok_copy[a, h].start()
 
+    loads[2].wait()
+    cotT[:, pl.ds(0, 128)] = dot(eye, cot[...], 1, 1).astype(BF16)
+    cot_copy.wait_recv()
+    cotT[:, pl.ds(128, 128)] = dot(eye, C2[...], 1, 1).astype(BF16)
+
+    def grad(xl, a, h):
+        wait(T.at[xl, h, pl.ds(0, 128)], tl_sem.at[a, h])
+        tok_copy[a, h].wait_recv()
+
+        def tile(i, carry):
+            at = pl.ds(pl.multiple_of(i * 512, 512), 512)
+            G[xl, h, :, at] = dot(cotT[...], T[xl, h, :, at], 1, 0).astype(BF16)
+            return carry
+
+        lax.fori_loop(0, SPAN // 512, tile, 0)
+
+    def piece(j, k, h):
+        return (lax.rem(x + j, NX), lax.rem(y + k, NY)) if h == 0 else (lax.rem(x + k, NX), lax.rem(y + j, NY))
+
+    def over(k, h):
+        return dev(dy=k) if h == 0 else dev(dx=k)
+
+    def send_grad(a, h):
+        if h == 0:
+            pairs = [(j, k) for j in ((1, 3), (2, 0))[a] for k in (2, 1, 3)]
+        else:
+            pairs = [(0, k) for k in ((1, 3), (2,))[a]]
+        for j, k in pairs:
+            xx, yy = piece(j, k, h)
+            if h == 0:
+                here, there = rows(xx, yy), pl.ds(COLS * j, COLS)
+            else:
+                here, there = pl.ds(pl.multiple_of(NY * COLS * (xx // 2), NY * COLS), NY * COLS), pl.ds(0, NY * COLS)
+            remote(
+                G.at[lax.rem(xx, 2), h, here], R1.at[h, k - 1, there], r1s_sem, r1r_sem.at[h, k - 1, j], over(k, h)
+            ).start()
+
+    grad(*chunks[0])
+    send_grad(*chunks[0][1:])
+
     pl.semaphore_wait(n_sem, 2)
 
     def onward(h, i, k):
@@ -134,39 +184,7 @@
                 onward(h, 0, 8).start()
                 onward(h, 1, 24).start()
 
-    cotT[:, pl.ds(0, 128)] = dot(eye, cot[...], 1, 1).astype(BF16)
-    cot_copy.wait_recv()
-    cotT[:, pl.ds(128, 128)] = dot(eye, C2[...], 1, 1).astype(BF16)
-
-    def grad(xl, a, h):
-        wait(T.at[xl, h, pl.ds(0, 128)], tl_sem.at[a, h])
-        tok_copy[a, h].wait_recv()
-
-        def tile(i, carry):
-            at = pl.ds(pl.multiple_of(i * 512, 512), 512)
-            G[xl, h, :, at] = dot(cotT[...], T[xl, h, :, at], 1, 0).astype(BF16)
-            return carry
-
-        lax.fori_loop(0, SPAN // 512, tile, 0)
-
-    def piece(j, k, h):
-        return (lax.rem(x + j, NX), lax.rem(y + k, NY)) if h == 0 else (lax.rem(x + k, NX), lax.rem(y + j, NY))
-
-    def over(k, h):
-        return dev(dy=k) if h == 0 else dev(dx=k)
-
-    def send_grad(a, h):
-        if h == 0:
-            pairs = [(j, k) for j in ((1, 3), (2, 0))[a] for k in (2, 1, 3)]
-        else:
-            pairs = [(j, k) for j in (1, 3, 2, 0) for k in ((1, 3), (2,))[a]]
-        for j, k in pairs:
-            xx, yy = piece(j, k, h)
-            remote(
-                G.at[lax.rem(xx, 2), h, rows(xx, yy)], R1.at[h, k - 1, j], r1s_sem, r1r_sem.at[h, k - 1, j], over(k, h)
-            ).start()
-
-    for xl, a, h in chunks:
+    for xl, a, h in chunks[1:]:
         grad(xl, a, h)
         send_grad(a, h)
 
@@ -177,46 +195,45 @@
             wait(Zb.at[res, h], z1r_sem.at[h])
             onward(h, 0, 8).start()
 
-    for h in range(2):
-
-        @pl.when(place[h] >= 2)
-        def _():
-            wait(Zb.at[res, h], z1r_sem.at[h])
-
-    for h, k in ((0, 4), (1, NZ - 4)):
-        remote(Zb.at[res, h], Zb.at[res, h], z2s_sem, z2r_sem.at[6 + h], dev(dz=k)).start()
-    for i, k in enumerate(near):
-        remote(Zb.at[res], Zb.at[res], z2s_sem, z2r_sem.at[i], dev(dz=k)).start()
+    first = jnp.where((place[0] == 0) | (place[0] == 3), 0, 1)
+
+    def place_of(h):
+        return jnp.where(h == 0, place[0], place[1])
+
+    def spread(h):
+        here = Zb.at[res, h]
+        remote(here, here, z2s_sem, z2r_sem.at[6, h], dev(dz=jnp.where(h == 0, 4, NZ - 4))).start()
+        for i, k in enumerate(near):
+            remote(here, here, z2s_sem, z2r_sem.at[i, h], dev(dz=k)).start()
+
+    @pl.when(place_of(first) == 3)
+    def _():
+        wait(Zb.at[res, first], z1r_sem.at[first])
+
+    spread(first)
+
+    @pl.when(place_of(1 - first) >= 2)
+    def _():
+        wait(Zb.at[res, 1 - first], z1r_sem.at[1 - first])
+
+    spread(1 - first)
 
     for h in range(2):
         for j in (1, 3, 2, 0):
             xx, yy = piece(j, 0, h)
             total = G[lax.rem(xx, 2), h, rows(xx, yy)].astype(F32)
+            there = pl.ds(COLS * j if h == 0 else pl.multiple_of(COLS * yy, COLS), COLS)
             for k in (1, 3, 2):
-                wait(R1.at[h, k - 1, j], r1r_sem.at[h, k - 1, j])
-                total += R1[h, k - 1, j].astype(F32)
+                if h == 0:
+                    wait(R1.at[h, k - 1, there], r1r_sem.at[h, k - 1, j])
+                elif j == 1:
+                    wait(R1.at[h, k - 1], r1r_sem.at[h, k - 1, 0])
+                total += R1[h, k - 1, there].astype(F32)
             if j == 0:
                 F0[h] = total
             else:
                 S1[h, j - 1] = total.astype(BF16)
                 remote(S1.at[h, j - 1], R2.at[h, j - 1], r2s_sem, r2r_sem.at[h, j - 1], over(j, 1 - h)).start()
-
-    for i, k in enumerate(near):
-        wait(Zb.at[lax.rem(res + 2 * RES - (k if k < RES else k - NZ), RES)], z2r_sem.at[i])
-    for h in range(2):
-        wait(Zb.at[lax.rem(res + 4, RES), h], z2r_sem.at[6 + h])
-    mine = rows(x, y)
-    for h in range(2):
-        for j in range(RES // 2):
-            at = 384 * j
-            W[x_lo, h, mine, at : at + 128] = Zb[2 * j, h, :, 0:128]
-            W[x_lo, h, mine, at + 128 : at + 256] = Zb[2 * j, h, :, 128:256] + Zb[2 * j + 1, h, :, 0:128]
-            W[x_lo, h, mine, at + 256 : at + 384] = Zb[2 * j + 1, h, :, 128:256]
-
-    for k in (1, 3, 2):
-        for h in range(2):
-            here = W.at[x_lo, h, mine]
-            remote(here, here, a1s_sem, a1r_sem.at[h, k - 1], over(k, 1 - h)).start()
 
     for h in range(2):
         total = F0[h]
@@ -232,6 +249,23 @@
         remote(Zs.at[lax.rem(res + 4, RES), h], Zr.at[6, h], q1s_sem, q1r_sem.at[6 + h], dev(dz=k)).start()
     for i, k in enumerate(near):
         remote(Zs.at[lax.rem(res + k, RES)], Zr.at[i], q1s_sem, q1r_sem.at[i], dev(dz=k)).start()
+    for h in range(2):
+        for i, k in enumerate(near):
+            wait(Zb.at[lax.rem(res + 2 * RES - (k if k < RES else k - NZ), RES), h], z2r_sem.at[i, h])
+        wait(Zb.at[lax.rem(res + 4, RES), h], z2r_sem.at[6, h])
+    mine = rows(x, y)
+    for h in range(2):
+        for j in range(RES // 2):
+            at = 384 * j
+            W[x_lo, h, mine, at : at + 128] = Zb[2 * j, h, :, 0:128]
+            W[x_lo, h, mine, at + 128 : at + 256] = Zb[2 * j, h, :, 128:256] + Zb[2 * j + 1, h, :, 0:128]
+            W[x_lo, h, mine, at + 256 : at + 384] = Zb[2 * j + 1, h, :, 128:256]
+
+    for k in (1, 3, 2):
+        for h in range(2):
+            here = W.at[x_lo, h, mine]
+            remote(here, here, a1s_sem, a1r_sem.at[h, k - 1], over(k, 1 - h)).start()
+
     def origin(j, k, h):
         return (mod(x - j, NX), mod(y - k, NY)) if h == 0 else (mod(x - k, NX), mod(y - j, NY))
 
@@ -239,13 +273,13 @@
         xx, yy = origin(j, k, h)
         return W.at[lax.rem(xx, 2), h, rows(xx, yy)]
 
-    for j in (0, 1, 3, 2):
-        for h in range(2):
-            here = part(j, 0, h)
-            if j:
-                wait(here, a1r_sem.at[h, j - 1])
-            for k in (1, 3, 2):
-                remote(here, here, a2s_sem, a2r_sem.at[h, k - 1, j], over(k, h)).start()
+    def pass_on(j, h):
+        here = part(j, 0, h)
+        for k in (1, 3, 2):
+            remote(here, here, a2s_sem, a2r_sem.at[h, k - 1, j], over(k, h)).start()
+
+    for h in range(2):
+        pass_on(0, h)
 
     for i in range(6):
         wait(Zr.at[i], q1r_sem.at[i])
@@ -277,14 +311,22 @@
         v_copy.start()
         Zr2[3] = own[...]
 
+    for j in (1, 3, 2):
+        for h in range(2):
+            wait(part(j, 0, h), a1r_sem.at[h, j - 1])
+            pass_on(j, h)
+
     acc = None
-    for h in range(2):
-        for k in (1, 3, 2):
-            for j in range(4):
-                wait(part(j, k, h), a2r_sem.at[h, k - 1, j])
-        for xl in range(2):
-            term = dot(T[xl, h], W[xl, h], 1, 1)
-            acc = term if acc is None else acc + term
+    for xl, h, pieces in (
+        (lax.rem(x_lo + 1, 2), 0, [(j, k) for j in (1, 3) for k in (1, 3, 2)]),
+        (lax.rem(x_lo + 1, 2), 1, [(j, k) for j in (0, 1, 3, 2) for k in (1, 3)]),
+        (x_lo, 0, [(j, k) for j in (0, 2) for k in (1, 3, 2)]),
+        (x_lo, 1, [(j, 2) for j in (0, 1, 3, 2)]),
+    ):
+        for j, k in pieces:
+            wait(part(j, k, h), a2r_sem.at[h, k - 1, j])
+        term = dot(T[xl, h], W[xl, h], 1, 1)
+        acc = term if acc is None else acc + term
     Psum[...] = acc
     p_copy = remote(Psum.at[pl.ds(128, 128)], Pr, p_sem.at[0], p_sem.at[1], sib)
     p_copy.start()
@@ -344,18 +386,21 @@
     projected, turned = pl.pallas_call(
         kernel,
         out_shape=(
-            jax.ShapeDtypeStruct((128, 128), BF16),
-            jax.ShapeDtypeStruct((8, ROWS), F32),
+            pltpu.VMEM((128, 128), BF16),
+            pltpu.VMEM((8, ROWS), F32),
         ),
-        in_specs=[pl.BlockSpec(memory_space=pltpu.HBM), vmem, vmem, vmem],
+        in_specs=[pl.BlockSpec(memory_space=pl.ANY)] * 4,
         out_specs=(vmem, vmem),
         scratch_shapes=[
+            pltpu.VMEM((8, ROWS), BF16),
+            pltpu.VMEM((8, block_scales.shape[0]), BF16),
+            pltpu.VMEM((128, 128), BF16),
             pltpu.VMEM((2, 2, 256, SPAN), BF16),
             pltpu.VMEM((128, 128), BF16),
             pltpu.VMEM((128, 256), BF16),
             pltpu.VMEM((2, 2, 128, SPAN), BF16),
             pltpu.VMEM((2, 2, 128, SPAN), BF16),
-            pltpu.VMEM((2, 3, 4, COLS, SPAN), BF16),
+            pltpu.VMEM((2, 3, NY * COLS, SPAN), BF16),
             pltpu.VMEM((2, 3, COLS, SPAN), BF16),
             pltpu.VMEM((2, 3, COLS, SPAN), BF16),
             pltpu.VMEM((2, COLS, SPAN), F32),
@@ -368,6 +413,7 @@
             pltpu.VMEM((4, COLS, PAD), BF16),
             pltpu.VMEM((256, 128), F32),
             pltpu.VMEM((128, 128), F32),
+            dma((3,)),
             dma((2, 2)),
             dma((2, 2)),
             dma((2, 2)),
@@ -379,7 +425,7 @@
             dma((2, 2)),
             dma((2,)),
             dma,
-            dma((8,)),
+            dma((7, 2)),
             dma,
             dma((2, 3, 4)),
             dma,
@@ -394,7 +440,7 @@
             dma((3,)),
         ],
         compiler_params=pltpu.CompilerParams(
-            collective_id=0, has_side_effects=True, vmem_limit_bytes=52 * 1024 * 1024
+            collective_id=0, has_side_effects=True, vmem_limit_bytes=60 * 1024 * 1024
         ),
     )(tokens, weight_codes.T, block_scales.T, cotangent)
     return projected, turned.T

time: 65.9 us -> 64.4 us (0.977)
  local copies, waits for them, and re-layouts: 3.33 us -> 1.22 us
  Pallas kernels: 61.7 us -> 62.4 us
    unnamed x8 -> x2, local copies, waits for them, and re-layouts: 3.33 us -> 1.22 us
    pallas_call x1, Pallas kernels: 61.7 us -> 62.4 us  [on_device(): pl.pallas_call(kernel, out_shape=(pltpu.VMEM((128, 128), BF16), pltpu.VME...]
where the time goes in v3:
time: 64.4 us; the launch traced here: 64.3 us
  Pallas kernels  62.4 us (97%)
  local copies, waits for them, and re-layouts  1.22 us (2%)
    pallas_call x1, Pallas kernels, on_device(): pl.pallas_call(kernel, out_shape=(pltpu.VMEM((128, 128), BF16), pltpu.VME...  62.4 us

profile of v3, /device:TPU:1, one launch (start us, length us, event | category | flops | bytes accessed | tf_op | source)
XLA Modules:
  0.0 64.3 jit_solution(1256781249643866627)
XLA Ops:
  0.6 62.4 %shard_map.59 = (bf16[128,128]{1,0:T(8,128)(2,1)S(1)}, f32[8,192]{1,0:T(8,128)S(1)}) custom-call(bf16[128,12288]{1,0:T(8,128)(2,1)} %tok_hbm.1, bf16[8,192]{1,0:T(8,128)(2,1)} %bitcast.4, bf16[8,96]{1,0:T(8,128)(2,1)} %bitcast.5, bf16[128,128]{1,0:T(8,128)(2,1)} %cot_hbm.1), custom_call_target="tpu_custom_call" | custom-call | tf_op jit(solution)/shard_map/pallas_call | solution.py:386
  63.1 0.6 copy.8
  63.7 0.6 copy.9

commit v4 on v3

--- a/solution.py
+++ b/solution.py
@@ -288,11 +288,14 @@
     total = Zs[res].astype(F32)
     for i in range(7):
         total += Zr[i].astype(F32)
-    Zq[...] = total.astype(BF16)
+    for h in range(2):
+        for c in range(2):
+            half = total[h, 8 * c : 8 * c + 8]
+            Zq[h, c] = jnp.concatenate([half[:, 0:128], half[:, 128:256]], 0).astype(BF16)
 
     def out_of(h, k, both):
         return remote(
-            Zq.at[h], Zr2.at[k - 1], q2s_sem.at[h, both], q2r_sem.at[k - 1], dev(dz=8 * k, sibling=both == 1)
+            Zq.at[h, 1 - core if both else core], Zr2.at[k - 1], q2s_sem.at[h, both], q2r_sem.at[k - 1], dev(dz=8 * k, sibling=both == 1)
         )
 
     for h in range(2):
@@ -303,13 +306,13 @@
                 out_of(h, k, 0).start()
                 out_of(h, k, 1).start()
 
-    own = Zq.at[lax.rem(octet, 2)]
-    v_copy = remote(own, Zr2.at[3], v_sem.at[0], v_sem.at[1], sib)
+    own = lax.rem(octet, 2)
+    v_copy = remote(Zq.at[own, 1 - core], Zr2.at[3], v_sem.at[0], v_sem.at[1], sib)
 
     @pl.when(lead)
     def _():
         v_copy.start()
-        Zr2[3] = own[...]
+        Zr2[3] = Zq[own, core]
 
     for j in (1, 3, 2):
         for h in range(2):
@@ -325,11 +328,14 @@
     ):
         for j, k in pieces:
             wait(part(j, k, h), a2r_sem.at[h, k - 1, j])
+        if acc is not None and len(pieces) == 4:
+            break
         term = dot(T[xl, h], W[xl, h], 1, 1)
         acc = term if acc is None else acc + term
-    Psum[...] = acc
+    Psum[128:256] = acc[128:256] + dot(T[xl, h, 128:256], W[xl, h], 1, 1)
     p_copy = remote(Psum.at[pl.ds(128, 128)], Pr, p_sem.at[0], p_sem.at[1], sib)
     p_copy.start()
+    Psum[0:128] = acc[0:128] + dot(T[xl, h, 0:128], W[xl, h], 1, 1)
 
     @pl.when(jnp.logical_not(lead))
     def _():
@@ -339,8 +345,8 @@
     for k in (1, 2, 3):
         wait(Zr2.at[k - 1], q2r_sem.at[k - 1])
         total += Zr2[k - 1].astype(F32)
-    picked = jnp.where(core == 0, total[0:8], total[8:16])
-    wg[...] = jnp.where(odd == 1, picked[:, 64:PAD], picked[:, 0:ROWS])
+    total = jnp.concatenate([total[0:8], total[8:16]], 1)
+    wg[...] = jnp.where(odd == 1, total[:, 64:PAD], total[:, 0:ROWS])
 
     p_copy.wait_recv()
     proj[...] = (Psum[0:128] + Pr[...]).astype(BF16)
@@ -368,8 +374,8 @@
 
         @pl.when(place[h] != 0)
         def _():
-            wait(Zq.at[h], q2s_sem.at[h, 0])
-            wait(Zq.at[h], q2s_sem.at[h, 1])
+            wait(Zq.at[h, 0], q2s_sem.at[h, 0])
+            wait(Zq.at[h, 1], q2s_sem.at[h, 1])
 
         @pl.when(place[h] == 0)
         def _():
@@ -409,8 +415,8 @@
             pltpu.VMEM((RES, 2, COLS, PAD), BF16),
             pltpu.VMEM((RES, 2, COLS, PAD), BF16),
             pltpu.VMEM((7, 2, COLS, PAD), BF16),
-            pltpu.VMEM((2, COLS, PAD), BF16),
-            pltpu.VMEM((4, COLS, PAD), BF16),
+            pltpu.VMEM((2, 2, COLS, 128), BF16),
+            pltpu.VMEM((4, COLS, 128), BF16),
             pltpu.VMEM((256, 128), F32),
             pltpu.VMEM((128, 128), F32),
             dma((3,)),

time: 64.4 us -> 64.3 us (level)
  no operation moved by 1% of the time
where the time goes in v4:
time: 64.3 us; the launch traced here: 64.1 us
  Pallas kernels  62.3 us (97%)
  local copies, waits for them, and re-layouts  1.22 us (2%)
    pallas_call x1, Pallas kernels, on_device(): pl.pallas_call(kernel, out_shape=(pltpu.VMEM((128, 128), BF16), pltpu.VME...  62.3 us

profile of v4, /device:TPU:1, one launch (start us, length us, event | category | flops | bytes accessed | tf_op | source)
XLA Modules:
  0.0 64.1 jit_solution(1403924870373233088)
XLA Ops:
  0.6 62.3 %shard_map.59 = (bf16[128,128]{1,0:T(8,128)(2,1)S(1)}, f32[8,192]{1,0:T(8,128)S(1)}) custom-call(bf16[128,12288]{1,0:T(8,128)(2,1)} %tok_hbm.1, bf16[8,192]{1,0:T(8,128)(2,1)} %bitcast.4, bf16[8,96]{1,0:T(8,128)(2,1)} %bitcast.5, bf16[128,128]{1,0:T(8,128)(2,1)} %cot_hbm.1), custom_call_target="tpu_custom_call" | custom-call | tf_op jit(solution)/shard_map/pallas_call | solution.py:392
  62.9 0.6 copy.8
  63.5 0.6 copy.9
